TPU v7x, 512 devices: a whole 4x4x16 slice. The times are simulated.
512 devices in a mesh: rep: 16 (over z), ep: 32 (over y, x, core).
Axes of the slice: x: 4, y: 4, z: 16, core: 2. Of those that a mesh axis runs over, the one named last changes fastest.
Arguments:
- tokens: bfloat16 [2048, 4096], P('rep'), may hold values from -6 to 6
- routes: int32 [2048, 2], P('rep'), may hold values from 0 to 7, all different within a row; in each aligned block of 128 rows (0 to 127, 128 to 255, ...) at most 64 rows name the same one
- gates: bfloat16 [2048, 2], P('rep'), may hold values from 0.19921875 to 1
- w_gate: bfloat16 [32, 1792, 4096], P('ep', 'rep'), may hold values from -0.09375 to 0.09375
- w_up: bfloat16 [32, 1792, 4096], P('ep', 'rep'), may hold values from -0.09375 to 0.09375
- direction: bfloat16 [32, 1792, 4096], P('ep', None, 'rep'), may hold values from -32 to 32
Outputs:
- next_direction: bfloat16 [32, 1792, 4096], P('ep', None, 'rep')
- rayleigh: float32 [1], replicated
Inputs may be any that keep to these rules, and one draw needn't show every extreme that they name: `routes`: each row names two different experts. In each aligned block of 128 rows (the tokens of one replica) no expert is named by more than 64 rows, and in some block some expert is named by exactly 64 rows.
All inputs are finite; a program needn't handle non-finite values.
Results may differ from a plain program's by a relative error of at most 0.007.
Values may be sent and summed in bfloat16 or wider, within the bound.
A program may use at most 64 MiB of HBM per device.

v0:
```python
import jax
import jax.numpy as jnp
from jax import lax
from jax.sharding import PartitionSpec as P

D = 4096
FF = 7168
EXPERTS = 8
ITERS = 2
CAP = 64


def own_slots(route_rows, expert, depth):
    pairs = route_rows.reshape(-1)
    hits = (pairs == expert).astype(jnp.int32)
    rank = jnp.cumsum(hits) - hits
    slots = jnp.arange(depth, dtype=jnp.int32)[:, None]
    return ((slots == rank[None, :]) & (hits[None, :] > 0)).astype(jnp.float32)


def on_device(tokens, routes, gates, w_gate, w_up, direction):
    n_rep = lax.axis_size("rep")
    n_ep = lax.axis_size("ep")
    slices = n_ep // EXPERTS
    local = tokens.shape[0]
    depth = CAP
    expert = lax.axis_index("ep") // slices
    route_all = lax.all_gather(routes, "rep", axis=0, tiled=True).reshape(n_rep, local, 2)
    tables = jax.vmap(lambda chosen: own_slots(chosen, expert, depth))(route_all)
    token_map = tables.reshape(n_rep, depth, local, 2).sum(axis=3)
    own_table = lax.dynamic_index_in_dim(tables, lax.axis_index("rep"), 0, keepdims=False)
    own_tokens = own_table.reshape(depth, local, 2).sum(axis=2)
    picked = jnp.dot(
        own_tokens.astype(jnp.bfloat16), tokens, preferred_element_type=jnp.float32
    ).astype(jnp.bfloat16)
    picked_gate = jnp.dot(
        own_table, gates.reshape(-1).astype(jnp.float32), precision=lax.Precision.HIGHEST
    ).astype(jnp.bfloat16)
    rows, rates = (
        lax.all_gather(picked, "rep", axis=0, tiled=True),
        lax.all_gather(picked_gate, "rep", axis=0, tiled=True),
    )
    contract = (((1,), (1,)), ((), ()))
    pre_gate = lax.dot_general(w_gate[0], rows, contract, preferred_element_type=jnp.float32)
    pre_up = lax.dot_general(w_up[0], rows, contract, preferred_element_type=jnp.float32)
    gated = (jax.nn.silu(pre_gate) * pre_up * rates.astype(jnp.float32)[None, :]).astype(
        jnp.bfloat16
    )
    hidden_t = lax.all_gather(gated, "rep", axis=0, tiled=True)
    current = direction[0]
    columns = current.shape[1]
    count = float(EXPERTS * FF * D)
    rayleigh = jnp.zeros((), jnp.float32)
    first_dims = (((0,), (0,)), ((), ()))
    for step in range(ITERS):
        partial_value = lax.dot_general(
            hidden_t, current, first_dims, preferred_element_type=jnp.float32
        ).reshape(n_rep, depth, columns)
        spread = jnp.einsum(
            "rst,rsd->rtd", token_map, partial_value, precision=lax.Precision.HIGHEST
        ).reshape(n_rep * local, columns)
        tangent = lax.psum_scatter(spread, "ep", scatter_dimension=0, tiled=True)
        piece = tangent.astype(jnp.bfloat16)
        sent = lax.all_gather(piece, "ep", axis=0, tiled=True)
        current_f = current.astype(jnp.float32)
        arrived = jnp.einsum(
            "rst,rtd->rsd",
            token_map.astype(jnp.bfloat16),
            sent.reshape(n_rep, local, columns),
            preferred_element_type=jnp.float32,
        ).astype(jnp.bfloat16)
        product = (
            jnp.dot(
                hidden_t,
                arrived.reshape(n_rep * depth, columns),
                preferred_element_type=jnp.float32,
            )
            / n_rep
        )
        energy, cross, square = lax.psum(
            (
                jnp.sum(product * product),
                jnp.sum(current_f * product),
                jnp.sum(current_f * current_f),
            ),
            ("rep", "ep"),
        )
        rayleigh = cross / count / (square / count + 1e-06)
        current = (product * lax.rsqrt(energy / count + 1e-06)).astype(jnp.bfloat16)
    return (current[None], rayleigh.reshape(1))


def solution(mesh):
    return jax.shard_map(
        on_device,
        mesh=mesh,
        in_specs=(
            P("rep", None),
            P("rep", None),
            P("rep", None),
            P("ep", "rep", None),
            P("ep", "rep", None),
            P("ep", None, "rep"),
        ),
        out_specs=(P("ep", None, "rep"), P()),
        check_vma=False,
    )
```

profile of v0, /device:TPU:1, one launch (start us, length us, event | category | flops | bytes accessed | tf_op | source)
XLA Modules:
  0.0 805.5 jit_solution(234640360543273105)
XLA Ops:
  7.2 29.7 %all_gather.18 = s32[2048,2]{0,1:T(2,128)S(1)} all-gather(s32[128,2]{0,1:T(2,128)} %param.7), channel_id=1, replica_groups=mesh['rep'=16,'ep'=32] {'rep'}, dimensions={0}, use_global_device_ids=true | all-gather | bytes 17408 | tf_op jit(solution)/shard_map/all_gather | solution.py:28
  39.3 1.4 fusion
  44.7 20.1 %all-reduce = bf16[1024]{0:T(1024)(128)(2,1)S(1)} all-reduce(bf16[1024]{0:T(1024)(128)(2,1)S(1)} %dynamic-update-slice), channel_id=1, replica_groups=mesh['rep'=16,'ep'=32] {'rep'}, use_global_device_ids=true, to_apply=%add | all-reduce | flops 1024 | bytes 4096
  64.8 86.5 %all-gather.5.cloned.1.call-done = bf16[1024,4096]{1,0:T(8,128)(2,1)} async-done(((bf16[64,4096]{1,0:T(8,128)(2,1)}), bf16[1024,4096]{1,0:T(8,128)(2,1)}) %all-gather.5.cloned.1.call-update) | async-done | bytes 8388624 | tf_op jit(solution)/shard_map/all_gather | solution.py:40
  151.3 6.4 convolution_bitcast_fusion.1
  157.7 3.5 fusion.5
  162.1 66.3 %all-gather.7.cloned.1.call-done = bf16[1792,1024]{1,0:T(8,128)(2,1)} async-done(((bf16[112,1024]{1,0:T(8,128)(2,1)}), bf16[1792,1024]{1,0:T(8,128)(2,1)}) %all-gather.7.cloned.1.call-update) | async-done | bytes 3670032 | tf_op jit(solution)/shard_map/all_gather | solution.py:49
  228.3 6.0 copy.60
  234.4 3.2 fusion.9
  237.5 3.2 fusion.20
  240.8 105.8 %reduce-scatter.3.cloned.1.call-done = f32[64,256]{1,0:T(8,128)} async-done(((f32[2048,256]{1,0:T(8,128)}), f32[64,256]{1,0:T(8,128)}) %reduce-scatter.3.cloned.1.call-update) | async-done | bytes 65552 | tf_op jit(solution)/shard_map/reduce_scatter | solution.py:62
  346.6 1.5 convert_element_type.87
  348.3 61.5 %all-gather.9.cloned.1.call-done = bf16[2048,256]{1,0:T(8,128)(2,1)} async-done(((bf16[64,256]{1,0:T(8,128)(2,1)}), bf16[2048,256]{1,0:T(8,128)(2,1)}) %all-gather.9.cloned.1.call-update) | async-done | bytes 1048592 | tf_op jit(solution)/shard_map/all_gather | solution.py:64
  409.8 1.5 convolution_convert_fusion.2
  411.3 3.8 multiply_reduce_fusion.1
  415.1 103.6 %psum.28 = f32[]{:T(128)} all-reduce(f32[]{:T(128)} %get-tuple-element.8), channel_id=1, replica_groups=mesh['rep'=16,'ep'=32] {'rep','ep'}, use_global_device_ids=true, to_apply=%region_6.7 | all-reduce | flops 1 | bytes 8 | tf_op jit(solution)/shard_map/psum | solution.py:80
  519.4 3.2 fusion.19
  522.6 3.2 fusion.21
  526.0 95.4 %reduce-scatter.5.cloned.1.call-done = f32[64,256]{1,0:T(8,128)} async-done(((f32[2048,256]{1,0:T(8,128)}), f32[64,256]{1,0:T(8,128)}) %reduce-scatter.5.cloned.1.call-update) | async-done | bytes 65552 | tf_op jit(solution)/shard_map/reduce_scatter | solution.py:62
  621.3 1.5 convert_element_type.90
  622.8 61.7 %all-gather.11.cloned.1.call-done = bf16[2048,256]{1,0:T(8,128)(2,1)} async-done(((bf16[64,256]{1,0:T(8,128)(2,1)}), bf16[2048,256]{1,0:T(8,128)(2,1)}) %all-gather.11.cloned.1.call-update) | async-done | bytes 1048592 | tf_op jit(solution)/shard_map/all_gather | solution.py:64
  684.5 1.5 convolution_convert_fusion.1
  686.1 4.6 fusion.1
  690.6 103.8 %all-reduce.1 = (f32[]{:T(128)}, f32[]{:T(128)}, f32[]{:T(128)}) all-reduce(f32[]{:T(128)} %get-tuple-element.3, f32[]{:T(128)} %get-tuple-element.2, f32[]{:T(128)} %get-tuple-element.4), channel_id=1, replica_groups=mesh['rep'=16,'ep'=32] {'rep','ep'}, use_global_device_ids=true, to_apply=%region_9.10 | all-reduce | flops 3 | bytes 24 | tf_op jit(solution)/shard_map/psum | solution.py:80
  (59 shorter events, 7.9 us)
Async XLA Ops:
  7.2 33.8 %copy-start = (bf16[128,4096]{1,0:T(8,128)(2,1)S(1)}, bf16[128,4096]{1,0:T(8,128)(2,1)}, u32[]{:S(2)}) copy-start(bf16[128,4096]{1,0:T(8,128)(2,1)} %param.6) | copy-start | bytes 3145732
  7.2 144.1 %all-gather.5.cloned.1.call-start = ((), (), s32[]{:S(2)}) async-start(), calls=%async_computation.2 | async-start | bytes 8912896 | tf_op jit(solution)/shard_map/all_gather | solution.py:40
  37.9 4.2 copy-start.1
  38.0 113.3 %copy-start.3 = (bf16[1,112,4096]{2,1,0:T(8,128)(2,1)S(1)}, bf16[1,112,4096]{2,1,0:T(8,128)(2,1)}, u32[]{:S(2)}) copy-start(bf16[1,112,4096]{2,1,0:T(8,128)(2,1)} %param.9) | copy-start | bytes 2752516
  42.1 186.2 %all-gather.7.cloned.1.call-start = ((), (), s32[]{:S(2)}) async-start(), calls=%async_computation.3 | async-start | bytes 3899392 | tf_op jit(solution)/shard_map/all_gather | solution.py:49
  151.3 6.4 copy-start.2
  151.3 6.4 copy-start.4
  161.3 185.3 %reduce-scatter.3.cloned.1.call-start = ((), (), s32[]{:S(2)}) async-start(), calls=%async_computation.4 | async-start | bytes 2162688 | tf_op jit(solution)/shard_map/reduce_scatter | solution.py:62
  228.3 6.0 copy-start.5
  240.8 169.0 %all-gather.9.cloned.1.call-start = ((), (), s32[]{:S(2)}) async-start(), calls=%async_computation.5 | async-start | bytes 1081344 | tf_op jit(solution)/shard_map/all_gather | solution.py:64
  348.1 273.2 %reduce-scatter.5.cloned.1.call-start = ((), (), s32[]{:S(2)}) async-start(), calls=%async_computation.6 | async-start | bytes 2162688 | tf_op jit(solution)/shard_map/reduce_scatter | solution.py:62
  415.1 107.5 %copy-start.6 = (f32[1792,256]{1,0:T(8,128)}, f32[1792,256]{1,0:T(8,128)S(1)}, u32[]{:S(2)}) copy-start(f32[1792,256]{1,0:T(8,128)S(1)} %get-tuple-element.9) | copy-start | bytes 5505028
  525.9 158.6 %all-gather.11.cloned.1.call-start = ((), (), s32[]{:S(2)}) async-start(), calls=%async_computation.7 | async-start | bytes 1081344 | tf_op jit(solution)/shard_map/all_gather | solution.py:64
Sparse Core Ops, SparseCore 0:
  42.2 109.0 all-gather.4
  161.4 66.8 all-gather.6
  240.9 105.6 reduce-scatter.2
  350.2 59.5 all-gather.8
  526.0 95.2 reduce-scatter.4
  624.9 59.5 all-gather.10
where the time goes:
time: 806 us
  waiting for transfers between devices  477 us (59%)
  blocking collectives  257 us (32%)
  matrix products  35.4 us (4%)
  between operations  18.9 us (2%)
  local copies, waits for them, and re-layouts  9.84 us (1%)
    psum x2, blocking collectives, on_device(): lax.psum((jnp.sum(product * product), jnp.sum(current_f * product), jnp.s...  207 us
    reduce_scatter x2, waiting for transfers between devices, on_device(): tangent = lax.psum_scatter(spread, 'ep', scatter_dimension=0, tiled=True)  201 us
    all_gather x2, waiting for transfers between devices, on_device(): sent = lax.all_gather(piece, 'ep', axis=0, tiled=True)  123 us
    all_gather x1, waiting for transfers between devices, on_device(): lax.all_gather(picked, 'rep', axis=0, tiled=True)  86.5 us
    all_gather x1, waiting for transfers between devices, on_device(): hidden_t = lax.all_gather(gated, 'rep', axis=0, tiled=True)  66.3 us
    all_gather x1, blocking collectives, on_device(): lax.all_gather(routes, 'rep', axis=0, tiled=True).reshape(n_rep, local, 2)  29.7 us
    unnamed x1, blocking collectives  20.1 us
  transfers between devices with their start and end apart: 6, of which 6 were waited for; matrix products, arithmetic and copies ran while one was open for 0% of the time, Pallas kernels for 0%

commit v1 on v0

--- a/solution.py
+++ b/solution.py
@@ -46,7 +46,9 @@
     gated = (jax.nn.silu(pre_gate) * pre_up * rates.astype(jnp.float32)[None, :]).astype(
         jnp.bfloat16
     )
-    hidden_t = lax.all_gather(gated, "rep", axis=0, tiled=True)
+    hidden_t = jnp.concatenate(
+        lax.all_to_all(jnp.stack([gated] * lax.axis_size("rep")), "rep", 0, 0), axis=0
+    )
     current = direction[0]
     columns = current.shape[1]
     count = float(EXPERTS * FF * D)

time: 806 us -> 904 us (1.12)
  waiting for transfers between devices: 477 us -> 565 us
    all_to_all x0 -> x1, waiting for transfers between devices: none -> 159 us  [on_device(): lax.all_to_all(jnp.stack([gated] * lax.axis_size('rep')), 'rep', 0, 0)]
    all_gather x1 -> x0, waiting for transfers between devices: 66.3 us -> none  [on_device(): hidden_t = lax.all_gather(gated, 'rep', axis=0, tiled=True)]
where the time goes in v1:
time: 904 us; the launch traced here: 903 us
  waiting for transfers between devices  565 us (62%)
  blocking collectives  257 us (28%)
  matrix products  34.7 us (4%)
  between operations  18.6 us (2%)
  local copies, waits for them, and re-layouts  12.2 us (1%)
    psum x2, blocking collectives, on_device(): lax.psum((jnp.sum(product * product), jnp.sum(current_f * product), jnp.s...  207 us
    reduce_scatter x2, waiting for transfers between devices, on_device(): tangent = lax.psum_scatter(spread, 'ep', scatter_dimension=0, tiled=True)  196 us
    all_to_all x1, waiting for transfers between devices, on_device(): lax.all_to_all(jnp.stack([gated] * lax.axis_size('rep')), 'rep', 0, 0)  159 us
    all_gather x2, waiting for transfers between devices, on_device(): sent = lax.all_gather(piece, 'ep', axis=0, tiled=True)  123 us
    all_gather x1, waiting for transfers between devices, on_device(): lax.all_gather(picked, 'rep', axis=0, tiled=True)  86.6 us
    all_gather x1, blocking collectives, on_device(): lax.all_gather(routes, 'rep', axis=0, tiled=True).reshape(n_rep, local, 2)  29.7 us
    unnamed x1, blocking collectives  20.1 us
  transfers between devices with their start and end apart: 6, of which 6 were waited for; matrix products, arithmetic and copies ran while one was open for 0% of the time, Pallas kernels for 0%

profile of v1, /device:TPU:1, one launch (start us, length us, event | category | flops | bytes accessed | tf_op | source)
XLA Modules:
  0.0 902.8 jit_solution(6173712533364615512)
XLA Ops:
  7.2 29.7 %all_gather.15 = s32[2048,2]{0,1:T(2,128)S(1)} all-gather(s32[128,2]{0,1:T(2,128)} %param.7), channel_id=1, replica_groups=mesh['rep'=16,'ep'=32] {'rep'}, dimensions={0}, use_global_device_ids=true | all-gather | bytes 17408 | tf_op jit(solution)/shard_map/all_gather | solution.py:28
  44.7 20.1 %all-reduce = bf16[1024]{0:T(1024)(128)(2,1)S(1)} all-reduce(bf16[1024]{0:T(1024)(128)(2,1)S(1)} %dynamic-update-slice), channel_id=1, replica_groups=mesh['rep'=16,'ep'=32] {'rep'}, use_global_device_ids=true, to_apply=%add | all-reduce | flops 1024 | bytes 4096
  64.8 86.6 %all-gather.4.cloned.1.call-done = bf16[1024,4096]{1,0:T(8,128)(2,1)} async-done(((bf16[64,4096]{1,0:T(8,128)(2,1)}), bf16[1024,4096]{1,0:T(8,128)(2,1)}) %all-gather.4.cloned.1.call-update) | async-done | bytes 8388624 | tf_op jit(solution)/shard_map/all_gather | solution.py:40
  151.3 6.4 convolution_bitcast_fusion.1
  157.7 2.8 fusion.5
  160.6 2.3 stack.2
  162.9 8.6 all-to-all-start
  172.3 158.5 %all-to-all-done = bf16[16,112,1024]{2,1,0:T(8,128)(2,1)} async-done(((bf16[16,112,1024]{2,1,0:T(8,128)(2,1)}), bf16[16,112,1024]{2,1,0:T(8,128)(2,1)}, u32[]{:S(2)}, u32[]{:S(2)}) %all-to-all-start) | async-done | bytes 3670048 | tf_op jit(solution)/shard_map/all_to_all | solution.py:50
  330.8 6.0 copy.60
  336.8 3.2 fusion.11
  340.0 3.3 fusion.21
  343.4 100.7 %reduce-scatter.3.cloned.1.call-done = f32[64,256]{1,0:T(8,128)} async-done(((f32[2048,256]{1,0:T(8,128)}), f32[64,256]{1,0:T(8,128)}) %reduce-scatter.3.cloned.1.call-update) | async-done | bytes 65552 | tf_op jit(solution)/shard_map/reduce_scatter | solution.py:64
  444.1 1.5 convert_element_type.87
  445.8 61.6 %all-gather.6.cloned.1.call-done = bf16[2048,256]{1,0:T(8,128)(2,1)} async-done(((bf16[64,256]{1,0:T(8,128)(2,1)}), bf16[2048,256]{1,0:T(8,128)(2,1)}) %all-gather.6.cloned.1.call-update) | async-done | bytes 1048592 | tf_op jit(solution)/shard_map/all_gather | solution.py:66
  507.4 1.5 convolution_convert_fusion.2
  508.9 3.8 multiply_reduce_fusion.1
  512.7 103.6 %psum.28 = f32[]{:T(128)} all-reduce(f32[]{:T(128)} %get-tuple-element.8), channel_id=1, replica_groups=mesh['rep'=16,'ep'=32] {'rep','ep'}, use_global_device_ids=true, to_apply=%region_6.7 | all-reduce | flops 1 | bytes 8 | tf_op jit(solution)/shard_map/psum | solution.py:82
  617.0 3.2 fusion.9
  620.2 3.2 fusion.22
  623.5 95.4 %reduce-scatter.5.cloned.1.call-done = f32[64,256]{1,0:T(8,128)} async-done(((f32[2048,256]{1,0:T(8,128)}), f32[64,256]{1,0:T(8,128)}) %reduce-scatter.5.cloned.1.call-update) | async-done | bytes 65552 | tf_op jit(solution)/shard_map/reduce_scatter | solution.py:64
  720.4 61.7 %all-gather.8.cloned.1.call-done = bf16[2048,256]{1,0:T(8,128)(2,1)} async-done(((bf16[64,256]{1,0:T(8,128)(2,1)}), bf16[2048,256]{1,0:T(8,128)(2,1)}) %all-gather.8.cloned.1.call-update) | async-done | bytes 1048592 | tf_op jit(solution)/shard_map/all_gather | solution.py:66
  782.1 1.5 convolution_convert_fusion.1
  783.6 4.6 fusion.1
  788.1 103.8 %all-reduce.1 = (f32[]{:T(128)}, f32[]{:T(128)}, f32[]{:T(128)}) all-reduce(f32[]{:T(128)} %get-tuple-element.3, f32[]{:T(128)} %get-tuple-element.2, f32[]{:T(128)} %get-tuple-element.4), channel_id=1, replica_groups=mesh['rep'=16,'ep'=32] {'rep','ep'}, use_global_device_ids=true, to_apply=%region_9.10 | all-reduce | flops 3 | bytes 24 | tf_op jit(solution)/shard_map/psum | solution.py:82
  (59 shorter events, 10.7 us)
Async XLA Ops:
  7.2 33.8 %copy-start = (bf16[128,4096]{1,0:T(8,128)(2,1)S(1)}, bf16[128,4096]{1,0:T(8,128)(2,1)}, u32[]{:S(2)}) copy-start(bf16[128,4096]{1,0:T(8,128)(2,1)} %param.6) | copy-start | bytes 3145732
  7.2 144.1 %all-gather.4.cloned.1.call-start = ((), (), s32[]{:S(2)}) async-start(), calls=%async_computation.3 | async-start | bytes 8912896 | tf_op jit(solution)/shard_map/all_gather | solution.py:40
  37.8 4.3 copy-start.2
  37.8 113.5 %copy-start.4 = (bf16[1,112,4096]{2,1,0:T(8,128)(2,1)S(1)}, bf16[1,112,4096]{2,1,0:T(8,128)(2,1)}, u32[]{:S(2)}) copy-start(bf16[1,112,4096]{2,1,0:T(8,128)(2,1)} %param.9) | copy-start | bytes 2752516
  151.3 6.4 copy-start.3
  151.3 6.4 copy-start.5
  162.9 167.9 %all-to-all-start = ((bf16[16,112,1024]{2,1,0:T(8,128)(2,1)}), bf16[16,112,1024]{2,1,0:T(8,128)(2,1)}, u32[]{:S(2)}, u32[]{:S(2)}) async-start(bf16[16,112,1024]{2,1,0:T(8,128)(2,1)} %stack.2), calls=%async_computation | async-start | bytes 7340032 | tf_op jit(solution)/shard_map/all_to_all | solution.py:50
  171.5 272.6 %reduce-scatter.3.cloned.1.call-start = ((), (), s32[]{:S(2)}) async-start(), calls=%async_computation.4 | async-start | bytes 2162688 | tf_op jit(solution)/shard_map/reduce_scatter | solution.py:64
  330.8 6.0 copy-start.6
  343.3 164.1 %all-gather.6.cloned.1.call-start = ((), (), s32[]{:S(2)}) async-start(), calls=%async_computation.5 | async-start | bytes 1081344 | tf_op jit(solution)/shard_map/all_gather | solution.py:66
  445.5 273.3 %reduce-scatter.5.cloned.1.call-start = ((), (), s32[]{:S(2)}) async-start(), calls=%async_computation.6 | async-start | bytes 2162688 | tf_op jit(solution)/shard_map/reduce_scatter | solution.py:64
  512.7 107.5 %copy-start.1 = (f32[1792,256]{1,0:T(8,128)}, f32[1792,256]{1,0:T(8,128)S(1)}, u32[]{:S(2)}) copy-start(f32[1792,256]{1,0:T(8,128)S(1)} %get-tuple-element.9) | copy-start | bytes 5505028
  623.5 158.6 %all-gather.8.cloned.1.call-start = ((), (), s32[]{:S(2)}) async-start(), calls=%async_computation.7 | async-start | bytes 1081344 | tf_op jit(solution)/shard_map/all_gather | solution.py:66
Sparse Core Ops, SparseCore 0:
  42.2 109.0 all-gather.3
  343.4 100.5 reduce-scatter.2
  447.8 59.5 all-gather.5
  623.6 95.2 reduce-scatter.4
  722.4 59.5 all-gather.7
